TPU v7x, 768 devices: a whole 4x8x12 slice. The times are simulated.
768 devices in a mesh: dp: 48 (over y_lo, z), ctx: 16 (over x, y_hi, core).
Axes of the slice: x: 4, y: 8 (y_hi: 2, y_lo: 4; y = y_hi * 4 + y_lo), z: 12, core: 2. Of those that a mesh axis runs over, the one named last changes fastest.
Arguments:
- q_gate: bfloat16 [48, 2048, 2048], P('dp', None, 'ctx'), may hold values from -6 to 6
- k_gate: bfloat16 [48, 2048, 2048], P('dp', None, 'ctx'), may hold values from -6 to 6
- values: bfloat16 [48, 2048, 2048], P('dp', None, 'ctx'), may hold values from -6 to 6
- out_grad: bfloat16 [48, 2048, 2048], P('dp', None, 'ctx'), may hold values from -6 to 6
- decay: float32 [2048], replicated, may hold values from 0.3 to 3
Outputs:
- kernel_grad: float32 [2048, 2048], P(None, 'ctx')
All inputs are finite; a program needn't handle non-finite values.
Results may differ from a plain program's by a relative error of at most 0.0041.
Values may be sent and summed in bfloat16 or wider, within the bound.
No kernel may reach another device: no remote copies, remote signals or barrier semaphores. Data moves between devices by JAX's collectives and lax.ppermute only.
A program may use at most 32 MiB of HBM per device.

v0:
```python
import math

import jax
import jax.numpy as jnp
from jax import lax
from jax.sharding import PartitionSpec as P

top_precision = lax.Precision.HIGHEST


def angle_table(row_ids, col_ids, modulus):
    index = row_ids[:, None] * col_ids[None, :] % modulus
    angle = 2.0 * math.pi / modulus * index.astype(jnp.float32)
    return (jnp.cos(angle), jnp.sin(angle))


def flat_dot(left, table):
    shaped = left.reshape((-1, left.shape[-1]))
    result = jnp.dot(shaped, table, precision=top_precision, preferred_element_type=jnp.float32)
    return result.reshape(left.shape[:-1] + (table.shape[1],))


def body(q_gate, k_gate, values, out_grad, decay):
    devs_ctx = lax.axis_size("ctx")
    devs_dp = lax.axis_size("dp")
    place = lax.axis_index("ctx")
    gated_in = (k_gate.astype(jnp.float32) * values.astype(jnp.float32)).astype(jnp.bfloat16)[0]
    gated_grad = (q_gate.astype(jnp.float32) * out_grad.astype(jnp.float32)).astype(jnp.bfloat16)[0]
    chans, span = gated_in.shape
    outer = 2 * devs_ctx
    total = outer * span
    outer_ids = jnp.arange(outer, dtype=jnp.int32)
    source_ids = jnp.arange(devs_ctx, dtype=jnp.int32)
    inner_index_list = jnp.arange(span, dtype=jnp.int32)
    outer_cosine, outer_sine = angle_table(outer_ids, source_ids, outer)
    inner_cos, inner_sin = angle_table(inner_index_list, inner_index_list, span)
    in_whole = lax.all_to_all(gated_in, "ctx", split_axis=0, concat_axis=1, tiled=True)
    grad_whole = lax.all_to_all(gated_grad, "ctx", split_axis=0, concat_axis=1, tiled=True)
    whole = jnp.stack([in_whole, grad_whole])
    local_ch = whole.shape[1]
    whole = whole.astype(jnp.float32).reshape((2, local_ch, devs_ctx, span))
    part_real = jnp.einsum("kp,scpb->sckb", outer_cosine, whole, precision=top_precision)
    part_imag = -jnp.einsum("kp,scpb->sckb", outer_sine, whole, precision=top_precision)
    full_cos, full_sin = angle_table(outer_ids, inner_index_list, total)
    halfway_real = part_real * full_cos + part_imag * full_sin
    half_imag = part_imag * full_cos - part_real * full_sin
    spec_real = flat_dot(halfway_real, inner_cos) + flat_dot(half_imag, inner_sin)
    spec_imag = flat_dot(half_imag, inner_cos) - flat_dot(halfway_real, inner_sin)
    prod_real = spec_real[0] * spec_real[1] + spec_imag[0] * spec_imag[1]
    prod_imag = spec_real[0] * spec_imag[1] - spec_imag[0] * spec_real[1]
    back_real = flat_dot(prod_real, inner_cos) - flat_dot(prod_imag, inner_sin)
    back_imag = flat_dot(prod_imag, inner_cos) + flat_dot(prod_real, inner_sin)
    rotated_real = back_real * full_cos - back_imag * full_sin
    rotated_imaginary = back_imag * full_cos + back_real * full_sin
    shard_lag_values = jnp.einsum(
        "rn,zrj->znj", outer_cosine, rotated_real, precision=top_precision
    )
    shard_lag_values = shard_lag_values - jnp.einsum(
        "rn,zrj->znj", outer_sine, rotated_imaginary, precision=top_precision
    )
    shard_lag_values = shard_lag_values.reshape((local_ch, devs_ctx * span)) / total
    shard_lag_values = lax.psum(shard_lag_values, "dp")
    owned = lax.all_to_all(shard_lag_values, "ctx", split_axis=1, concat_axis=0, tiled=True)
    seq_len = span * devs_ctx
    lag_ids = (place * span + jnp.arange(span, dtype=jnp.int32)).astype(jnp.float32)
    window = jnp.exp(-decay[:, None] * lag_ids[None, :] / seq_len)
    return owned * window / math.sqrt(devs_dp * seq_len)


def solution(mesh):
    return jax.shard_map(
        body,
        mesh=mesh,
        in_specs=(
            P("dp", None, "ctx"),
            P("dp", None, "ctx"),
            P("dp", None, "ctx"),
            P("dp", None, "ctx"),
            P(),
        ),
        out_specs=P(None, "ctx"),
        check_vma=False,
    )
```

profile of v0, /device:TPU:1, one launch (start us, length us, event | category | flops | bytes accessed | tf_op | source)
XLA Modules:
  0.0 596.3 jit_solution(5700091010937978992)
XLA Ops:
  6.5 2.2 multiply_convert_fusion
  8.8 13.9 %all-to-all-start.1 = ((bf16[16,128,128]{2,1,0:T(8,128)(2,1)}), bf16[16,128,128]{2,1,0:T(8,128)(2,1)S(1)}, u32[]{:S(2)}, u32[]{:S(2)}) async-start(bf16[16,128,128]{2,1,0:T(8,128)(2,1)} %bitcast.3), calls=%async_computation.1 | async-start | bytes 1048576 | tf_op jit(solution)/shard_map/all_to_all | solution.py:38
  22.6 0.0 copy-done.1
  22.6 0.0 copy-done
  22.7 0.9 multiply_convert_fusion.1
  23.6 14.1 %all-to-all-done.1 = bf16[16,128,128]{2,1,0:T(8,128)(2,1)S(1)} async-done(((bf16[16,128,128]{2,1,0:T(8,128)(2,1)}), bf16[16,128,128]{2,1,0:T(8,128)(2,1)S(1)}, u32[]{:S(2)}, u32[]{:S(2)}) %all-to-all-start.1) | async-done | bytes 524320 | tf_op jit(solution)/shard_map/all_to_all | solution.py:38
  37.7 7.6 %all-to-all-start = ((bf16[16,128,128]{2,1,0:T(8,128)(2,1)}), bf16[16,128,128]{2,1,0:T(8,128)(2,1)S(1)}, u32[]{:S(2)}, u32[]{:S(2)}) async-start(bf16[16,128,128]{2,1,0:T(8,128)(2,1)} %bitcast), calls=%async_computation | async-start | bytes 1048576 | tf_op jit(solution)/shard_map/all_to_all | solution.py:37
  45.3 0.0 all-reduce.2.cloned.1.call-start
  45.4 0.1 fusion.83
  45.4 0.3 copy.58
  45.8 13.2 %all-to-all-done = bf16[16,128,128]{2,1,0:T(8,128)(2,1)S(1)} async-done(((bf16[16,128,128]{2,1,0:T(8,128)(2,1)}), bf16[16,128,128]{2,1,0:T(8,128)(2,1)S(1)}, u32[]{:S(2)}, u32[]{:S(2)}) %all-to-all-start) | async-done | bytes 524320 | tf_op jit(solution)/shard_map/all_to_all | solution.py:37
  59.0 0.3 copy.59
  59.4 1.9 fusion.44
  61.3 2.8 fusion
  64.0 7.3 %fusion.4 = f32[2,128,32,128]{3,1,2,0:T(8,128)S(1)} fusion(f32[2,128,32,128]{3,2,1,0:T(8,128)S(1)} %get-tuple-element.6), kind=kOutput, calls=%fused_computation.8 | convolution fusion | flops 1610842112 | bytes 8388608 | tf_op jit(solution)/shard_map/dot_general | solution.py:19
  71.3 6.9 %fusion.2 = f32[2,128,32,128]{3,1,2,0:T(8,128)S(1)} fusion(f32[2,128,32,128]{3,2,1,0:T(8,128)S(1)} %get-tuple-element.6), kind=kOutput, calls=%fused_computation.6 | convolution fusion | flops 1610842112 | bytes 8388608 | tf_op jit(solution)/shard_map/dot_general | solution.py:19
  78.2 7.1 %fusion.10 = f32[2,128,32,128]{3,1,2,0:T(8,128)S(1)} fusion(f32[2,128,32,128]{3,1,2,0:T(8,128)S(1)} %fusion.4, f32[2,128,32,128]{3,2,1,0:T(8,128)S(1)} %get-tuple-element.5), kind=kOutput, calls=%fused_computation.14 | convolution fusion | flops 1611890688 | bytes 12582912 | tf_op jit(solution)/shard_map/dot_general | solution.py:19
  85.3 7.0 %fusion.13 = f32[2,128,32,128]{3,1,2,0:T(8,128)S(1)} fusion(f32[2,128,32,128]{3,1,2,0:T(8,128)S(1)} %fusion.2, f32[2,128,32,128]{3,2,1,0:T(8,128)S(1)} %get-tuple-element.5), kind=kOutput, calls=%fused_computation.15 | convolution fusion | flops 1611890688 | bytes 12582912 | tf_op jit(solution)/shard_map/dot_general | solution.py:19
  92.4 0.9 multiply_add_fusion.1
  93.2 2.4 fusion.18
  95.6 2.1 fusion.16
  97.7 2.2 fusion.28
  99.9 2.5 multiply_subtract_fusion
  102.3 2.4 fusion.24
  104.8 3.4 fusion.40
  108.2 0.0 all-reduce.2.cloned.1.call-update
  108.2 0.0 copy-start.2
  108.2 416.2 %all-reduce.2.cloned.1.call-done = f32[128,16,128]{2,1,0:T(8,128)} async-done(((f32[128,16,128]{2,1,0:T(8,128)}), f32[128,16,128]{2,1,0:T(8,128)}) %all-reduce.2.cloned.1.call-update) | async-done | bytes 1048592 | tf_op jit(solution)/shard_map/psum | solution.py:62
  524.4 2.5 copy.29
  526.9 41.2 %all-to-all-start.2 = ((f32[128,16,128]{2,0,1:T(8,128)}), f32[128,16,128]{2,0,1:T(8,128)S(1)}, u32[]{:S(2)}, u32[]{:S(2)}) async-start(f32[128,16,128]{2,0,1:T(8,128)} %copy.29), calls=%async_computation.2 | async-start | bytes 2097152 | tf_op jit(solution)/shard_map/all_to_all | solution.py:63
  568.2 19.6 %all-to-all-done.2 = f32[128,16,128]{2,0,1:T(8,128)S(1)} async-done(((f32[128,16,128]{2,0,1:T(8,128)}), f32[128,16,128]{2,0,1:T(8,128)S(1)}, u32[]{:S(2)}, u32[]{:S(2)}) %all-to-all-start.2) | async-done | bytes 1048608 | tf_op jit(solution)/shard_map/all_to_all | solution.py:63
  587.8 1.3 fusion.43
  (5 shorter events, 0.0 us)
Async XLA Ops:
  6.5 16.1 %copy-start.1 = (bf16[1,2048,128]{2,1,0:T(8,128)(2,1)S(1)}, bf16[1,2048,128]{2,1,0:T(8,128)(2,1)}, u32[]{:S(2)}) copy-start(bf16[1,2048,128]{2,1,0:T(8,128)(2,1)} %param.6) | copy-start | bytes 1572868
  6.5 16.1 %copy-start = (bf16[1,2048,128]{2,1,0:T(8,128)(2,1)S(1)}, bf16[1,2048,128]{2,1,0:T(8,128)(2,1)}, u32[]{:S(2)}) copy-start(bf16[1,2048,128]{2,1,0:T(8,128)(2,1)} %param.7) | copy-start | bytes 1572868
  8.8 29.0 %all-to-all-start.1 = ((bf16[16,128,128]{2,1,0:T(8,128)(2,1)}), bf16[16,128,128]{2,1,0:T(8,128)(2,1)S(1)}, u32[]{:S(2)}, u32[]{:S(2)}) async-start(bf16[16,128,128]{2,1,0:T(8,128)(2,1)} %bitcast.3), calls=%async_computation.1 | async-start | bytes 1048576 | tf_op jit(solution)/shard_map/all_to_all | solution.py:38
  37.7 21.3 %all-to-all-start = ((bf16[16,128,128]{2,1,0:T(8,128)(2,1)}), bf16[16,128,128]{2,1,0:T(8,128)(2,1)S(1)}, u32[]{:S(2)}, u32[]{:S(2)}) async-start(bf16[16,128,128]{2,1,0:T(8,128)(2,1)} %bitcast), calls=%async_computation | async-start | bytes 1048576 | tf_op jit(solution)/shard_map/all_to_all | solution.py:37
  45.3 479.1 %all-reduce.2.cloned.1.call-start = ((), (), s32[]{:S(2)}) async-start(), calls=%async_computation.3 | async-start | bytes 2097152 | tf_op jit(solution)/shard_map/psum | solution.py:62
  108.2 459.9 %copy-start.2 = (f32[2048]{0:T(1024)S(1)}, f32[2048]{0:T(1024)}, u32[]{:S(2)}) copy-start(f32[2048]{0:T(1024)} %param.9) | copy-start | bytes 24580
  526.9 60.8 %all-to-all-start.2 = ((f32[128,16,128]{2,0,1:T(8,128)}), f32[128,16,128]{2,0,1:T(8,128)S(1)}, u32[]{:S(2)}, u32[]{:S(2)}) async-start(f32[128,16,128]{2,0,1:T(8,128)} %copy.29), calls=%async_computation.2 | async-start | bytes 2097152 | tf_op jit(solution)/shard_map/all_to_all | solution.py:63
Sparse Core Ops, SparseCore 0:
  108.4 416.0 all-reduce.1
where the time goes:
time: 606 us; the launch traced here: 596 us
  waiting for transfers between devices  463 us (76%)
  starting transfers between devices  62.7 us (10%)
  matrix products  47.9 us (8%)
  between operations  13.9 us (2%)
    psum x1, waiting for transfers between devices, body(): shard_lag_values = lax.psum(shard_lag_values, 'dp')  416 us
    all_to_all x1, starting transfers between devices, body(): lax.all_to_all(shard_lag_values, 'ctx', split_axis=1, concat_axis=0, tile...  41.2 us
    dot_general x8, matrix products, flat_dot(): jnp.dot(shaped, table, precision=top_precision, preferred_element_type=jn...  37.4 us
    all_to_all x1, waiting for transfers between devices, body(): lax.all_to_all(shard_lag_values, 'ctx', split_axis=1, concat_axis=0, tile...  19.6 us
    all_to_all x1, waiting for transfers between devices, body(): lax.all_to_all(gated_grad, 'ctx', split_axis=0, concat_axis=1, tiled=True)  14.1 us
    all_to_all x1, starting transfers between devices, body(): lax.all_to_all(gated_grad, 'ctx', split_axis=0, concat_axis=1, tiled=True)  13.9 us
    all_to_all x1, waiting for transfers between devices, body(): lax.all_to_all(gated_in, 'ctx', split_axis=0, concat_axis=1, tiled=True)  13.2 us
  transfers between devices with their start and end apart: 4, of which 4 were waited for; matrix products, arithmetic and copies ran while one was open for 0% of the time, Pallas kernels for 0%

commit v1 on v0

v1 whole, which is shorter than its diff:
```python
import functools
import math

import jax
import jax.numpy as jnp
import ml_dtypes
import numpy as np
from jax import lax
from jax.experimental import pallas as pl
from jax.experimental.pallas import tpu as pltpu
from jax.sharding import Mesh, PartitionSpec as P

F32 = jnp.float32
BF16 = jnp.bfloat16

SPAN = 128
BLOCKS = 16
FREQS = BLOCKS + 1
PAD_FREQS = FREQS + 1
ROWS = 16
CHANS = ROWS // 2
OUTER = 2 * BLOCKS
TOTAL = OUTER * SPAN


def split16(table):
    high = table.astype(ml_dtypes.bfloat16)
    low = (table - high.astype(np.float64)).astype(ml_dtypes.bfloat16)
    return np.stack([high, low])


@functools.lru_cache(maxsize=None)
def tables():
    k = np.arange(FREQS)[:, None]
    p = np.arange(BLOCKS)[None, :]
    angle = 2.0 * np.pi * (k * p % OUTER) / OUTER
    outer = np.stack([np.cos(angle), -np.sin(angle)], axis=1)
    spread = np.einsum("kcp,rq->kcrpq", outer, np.eye(ROWS))
    spread = spread.reshape(FREQS * 2 * ROWS, BLOCKS * ROWS)
    b = np.arange(SPAN)
    angle = 2.0 * np.pi * (b[:, None] * b[None, :] % SPAN) / SPAN
    cos, sin = np.cos(angle), np.sin(angle)
    forward = np.block([[cos, -sin], [sin, cos]])
    backward = np.block([[cos, sin], [-sin, cos]])
    angle = 2.0 * np.pi * np.arange(PAD_FREQS)[:, None] * b[None, :] / TOTAL
    twist = np.stack([np.cos(angle), np.sin(angle)], axis=1)
    twist = np.broadcast_to(twist[:, :, None, :], (PAD_FREQS, 2, 8, SPAN))
    return (
        split16(spread),
        split16(forward),
        split16(backward),
        np.ascontiguousarray(twist.astype(np.float32)),
    )


def halves(x):
    high = x.astype(BF16)
    return high, (x - high.astype(F32)).astype(BF16)


def dot(a, b):
    return jnp.dot(a, b, preferred_element_type=F32)


def gate_kernel(k_ref, v_ref, q_ref, g_ref, out_ref):
    chans = k_ref.shape[1]
    first = k_ref[0].astype(F32) * v_ref[0].astype(F32)
    second = q_ref[0].astype(F32) * g_ref[0].astype(F32)
    shape = (chans // CHANS, CHANS, SPAN)
    both = jnp.concatenate([first.reshape(shape), second.reshape(shape)], axis=1)
    out_ref[...] = both.astype(BF16)


def gate(q_gate, k_gate, values, out_grad):
    chans = q_gate.shape[1]
    tile = min(chans, 512)
    spec = pl.BlockSpec((1, tile, SPAN), lambda i: (0, i, 0))
    return pl.pallas_call(
        gate_kernel,
        grid=(chans // tile,),
        in_specs=[spec] * 4,
        out_specs=pl.BlockSpec((tile // CHANS, ROWS, SPAN), lambda i: (i, 0, 0)),
        out_shape=jax.ShapeDtypeStruct((chans // CHANS, ROWS, SPAN), BF16),
        name="gate",
    )(k_gate, values, q_gate, out_grad)


def correlate_kernel(x_ref, outer_ref, fwd_ref, bwd_ref, twist_ref, out_ref, high_ref, low_ref):
    seqs = x_ref.shape[0]
    copies = out_ref.shape[0]
    cos = twist_ref[:, 0]
    sin = twist_ref[:, 1]

    def outer_step(s, carry):
        x = x_ref[s].reshape(BLOCKS * ROWS, SPAN)
        y = dot(outer_ref[0], x) + dot(outer_ref[1], x)
        y = y.reshape(FREQS, 2, 2, CHANS, SPAN)
        real, imag = y[:, 0], y[:, 1]
        c = cos[:FREQS, None]
        d = sin[:FREQS, None]
        turned_real = (real * c + imag * d).reshape(FREQS, ROWS, SPAN)
        turned_imag = (imag * c - real * d).reshape(FREQS, ROWS, SPAN)
        rows = pl.ds(pl.multiple_of(s * ROWS, ROWS), ROWS)
        high, low = halves(turned_real)
        high_ref[:, rows, :SPAN] = high
        low_ref[:, rows, :SPAN] = low
        high, low = halves(turned_imag)
        high_ref[:, rows, SPAN:] = high
        low_ref[:, rows, SPAN:] = low
        return carry

    lax.fori_loop(0, seqs, outer_step, 0, unroll=2 if seqs % 2 == 0 else 1)

    cross = []
    for k in range(FREQS):
        high = high_ref[k]
        spec = dot(high, fwd_ref[0]) + (dot(low_ref[k], fwd_ref[0]) + dot(high, fwd_ref[1]))
        spec = spec.reshape(seqs, 2, CHANS, 2 * SPAN)
        in_real, in_imag = spec[:, 0, :, :SPAN], spec[:, 0, :, SPAN:]
        grad_real, grad_imag = spec[:, 1, :, :SPAN], spec[:, 1, :, SPAN:]
        real = jnp.sum(in_real * grad_real + in_imag * grad_imag, axis=0)
        imag = jnp.sum(in_real * grad_imag - in_imag * grad_real, axis=0)
        cross.append(jnp.concatenate([real, imag], axis=1))
    cross.append(jnp.zeros((CHANS, 2 * SPAN), F32))
    cross = jnp.concatenate(cross, axis=0)

    high, low = halves(cross)
    back = dot(high, bwd_ref[0]) + (dot(low, bwd_ref[0]) + dot(high, bwd_ref[1]))
    back = back.reshape(PAD_FREQS, CHANS, 2 * SPAN)
    real, imag = back[:, :, :SPAN], back[:, :, SPAN:]
    turned_real = real * cos - imag * sin
    turned_imag = real * sin + imag * cos
    for n in range(BLOCKS):
        total = None
        for k in range(FREQS):
            weight = (1.0 if k in (0, BLOCKS) else 2.0) / TOTAL
            angle = 2.0 * math.pi * (k * n % OUTER) / OUTER
            term = turned_real[k] * (weight * math.cos(angle))
            if k * n % BLOCKS:
                term = term - turned_imag[k] * (weight * math.sin(angle))
            total = term if total is None else total + term
        for copy in range(copies):
            out_ref[copy, n] = total


def correlate(x, copies):
    seqs = x.shape[0]
    outer, forward, backward, twist = tables()
    rows = seqs * ROWS
    flops = 2 * seqs * 2 * outer.shape[1] * outer.shape[2] * SPAN + 6 * FREQS * rows * 4 * SPAN * SPAN
    return pl.pallas_call(
        correlate_kernel,
        in_specs=[pl.BlockSpec(memory_space=pltpu.VMEM)] * 5,
        out_specs=pl.BlockSpec(memory_space=pltpu.VMEM),
        out_shape=jax.ShapeDtypeStruct((copies, BLOCKS, CHANS, SPAN), F32),
        scratch_shapes=[
            pltpu.VMEM((FREQS, rows, 2 * SPAN), BF16),
            pltpu.VMEM((FREQS, rows, 2 * SPAN), BF16),
        ],
        compiler_params=pltpu.CompilerParams(vmem_limit_bytes=32 * 1024 * 1024),
        cost_estimate=pl.CostEstimate(flops=flops, bytes_accessed=3_000_000, transcendentals=0),
        name="correlate",
    )(x, outer, forward, backward, twist)


CTX = ("x", "y_hi", "core")
NEAR = ("y_lo", "z_lo")


def to_each(x, axes):
    return lax.all_to_all(x, axes, split_axis=0, concat_axis=0, tiled=True)


def body(length, batch, q_gate, k_gate, values, out_grad, decay):
    near = lax.axis_size(NEAR)
    far = lax.axis_size("z_hi")
    gated = gate(q_gate, k_gate, values, out_grad)
    whole = to_each(gated, NEAR + CTX)
    part = correlate(whole.reshape(near, BLOCKS, ROWS, SPAN), far)

    group = BLOCKS * CHANS
    mine = lax.dynamic_slice_in_dim(decay, lax.axis_index(NEAR) * group, group)
    lags = (lax.axis_index(CTX) * SPAN + jnp.arange(SPAN, dtype=jnp.int32)).astype(F32)
    window = jnp.exp(-mine[:, None] * lags[None, :] / length) / math.sqrt(batch * length)

    sent = part.reshape(far * BLOCKS, CHANS, SPAN)
    lag_parts = to_each(sent, ("z_hi",) + CTX).reshape(far, group, SPAN)
    ours = (jnp.sum(lag_parts, axis=0) * window).astype(BF16)
    everyone = to_each(jnp.broadcast_to(ours[None], (near, group, SPAN)), NEAR)
    return everyone.reshape(near * group, SPAN).astype(F32)


def solution(mesh):
    dp, ctx = mesh.devices.shape
    fine = Mesh(
        mesh.devices.reshape(4, dp // 16, 4, ctx // 4, 2, 2),
        ("y_lo", "z_hi", "z_lo") + CTX,
    )
    seqs = ("y_lo", "z_hi", "z_lo")
    return jax.shard_map(
        functools.partial(body, SPAN * ctx, dp),
        mesh=fine,
        in_specs=(P(seqs, None, CTX),) * 4 + (P(),),
        out_specs=P(None, CTX),
        check_vma=False,
    )
```

time: 606 us -> 117 us (0.19); the launches traced: 596 us -> 116 us
  waiting for transfers between devices: 463 us -> 17.4 us
  blocking collectives: 0 us -> 71.6 us
  starting transfers between devices: 62.7 us -> 14.5 us
  matrix products: 47.9 us -> 0 us
  between operations: 13.9 us -> 0.08 us
  Pallas kernels: 0 us -> 10.6 us
    psum x1 -> x0, waiting for transfers between devices: 416 us -> none  [body(): shard_lag_values = lax.psum(shard_lag_values, 'dp')]
    all_to_all x0 -> x2, blocking collectives: none -> 71.6 us  [to_each(): return lax.all_to_all(x, axes, split_axis=0, concat_axis=0, tiled=True)]
    all_to_all x3 -> x1, starting transfers between devices: 62.7 us -> 14.5 us  [to_each(): return lax.all_to_all(x, axes, split_axis=0, concat_axis=0, tiled=True)]
    dot_general x12 -> x0, matrix products: 47.9 us -> none  [the longest x8 37.4 us: flat_dot(): jnp.dot(shaped, table, precision=top_precision, preferred_element_type=jn...]
    all_to_all x3 -> x1, waiting for transfers between devices: 46.9 us -> 17.4 us  [to_each(): return lax.all_to_all(x, axes, split_axis=0, concat_axis=0, tiled=True)]
    pallas_call x0 -> x2, Pallas kernels: none -> 10.6 us  [the longest x1 6.94 us: correlate(): pl.pallas_call(correlate_kernel, in_specs=[pl.BlockSpec(memory_space=pltp...]
  transfers between devices with their start and end apart: 4 -> 1, of which waited for: 4 -> 1; matrix products, arithmetic and copies ran while one was open for 0% -> 1% of each run, Pallas kernels for 0% -> 0%
where the time goes in v1:
time: 117 us; the launch traced here: 116 us
  blocking collectives  71.6 us (61%)
  waiting for transfers between devices  17.4 us (15%)
  starting transfers between devices  14.5 us (12%)
  Pallas kernels  10.6 us (9%)
  other arithmetic  1.95 us (2%)
    all_to_all x2, blocking collectives, to_each(): return lax.all_to_all(x, axes, split_axis=0, concat_axis=0, tiled=True)  71.6 us
    all_to_all x1, waiting for transfers between devices, to_each(): return lax.all_to_all(x, axes, split_axis=0, concat_axis=0, tiled=True)  17.4 us
    all_to_all x1, starting transfers between devices, to_each(): return lax.all_to_all(x, axes, split_axis=0, concat_axis=0, tiled=True)  14.5 us
    pallas_call x1, Pallas kernels, correlate(): pl.pallas_call(correlate_kernel, in_specs=[pl.BlockSpec(memory_space=pltp...  6.94 us
    pallas_call x1, Pallas kernels, gate(): pl.pallas_call(gate_kernel, grid=(chans // tile,), in_specs=[spec] * 4, o...  3.69 us
  transfers between devices with their start and end apart: 1, of which 1 were waited for; matrix products, arithmetic and copies ran while one was open for 1% of the time, Pallas kernels for 0%

profile of v1, /device:TPU:1, one launch (start us, length us, event | category | flops | bytes accessed | tf_op | source)
XLA Modules:
  0.0 116.3 jit_solution(17932459495658386758)
XLA Ops:
  0.0 3.7 %gate.1 = bf16[256,16,128]{2,1,0:T(8,128)(2,1)} custom-call(bf16[1,2048,128]{2,1,0:T(8,128)(2,1)} %k_ref.1, bf16[1,2048,128]{2,1,0:T(8,128)(2,1)} %v_ref.1, bf16[1,2048,128]{2,1,0:T(8,128)(2,1)} %q_ref.1, bf16[1,2048,128]{2,1,0:T(8,128)(2,1)} %g_ref.1), custom_call_target="tpu_custom_call" | custom-call | tf_op jit(solution)/shard_map/gate/pallas_call | solution.py:78
  3.7 0.0 copy-start
  3.7 0.0 copy-start.1
  3.7 0.0 copy-start.2
  3.7 0.0 copy-start.3
  3.7 50.5 %all_to_all.15 = bf16[256,16,128]{2,1,0:T(8,128)(2,1)S(1)} all-to-all(bf16[256,16,128]{2,1,0:T(8,128)(2,1)} %gate.1), channel_id=1, replica_groups=mesh['y_lo'=4,'z_hi'=3,'z_lo'=4,'x'=4,'y_hi'=2,'core'=2] {'y_lo','z_lo',..., dimensions={0} | all-to-all | bytes 2097152 | tf_op jit(solution)/shard_map/all_to_all | solution.py:171
  54.2 0.0 copy-done
  54.2 0.0 copy-done.1
  54.2 0.0 copy-done.2
  54.2 0.0 copy-done.3
  54.2 6.9 %correlate.1 = f32[3,16,8,128]{3,2,1,0:T(8,128)} custom-call(bf16[16,16,16,128]{3,2,1,0:T(8,128)(2,1)S(1)} %bitcast.8, bf16[2,544,256]{2,1,0:T(8,128)(2,1)S(1)} %copy-done, bf16[2,256,256]{2,1,0:T(8,128)(2,1)S(1)} %copy-done.1, bf16[2,256,256]{2,1,0:T(8,128)(2,1)S(1)} %copy-done.2, f32[18,2,8,128]{3,2,1,0:T(8,128)S(1)} %copy-done.3), custom_call_target="tpu_custom_call" | custom-call | flops 2852126720 | bytes 3000000 | tf_op jit(solution)/shard_map/correlate/pallas_call | solution.py:151
  61.2 14.5 %all-to-all-start.1 = ((f32[48,8,128]{2,1,0:T(8,128)}), f32[48,8,128]{2,1,0:T(8,128)S(1)}, u32[]{:S(2)}, u32[]{:S(2)}) async-start(f32[48,8,128]{2,1,0:T(8,128)} %bitcast.1), calls=%async_computation.1 | async-start | bytes 393216 | tf_op jit(solution)/shard_map/all_to_all | solution.py:171
  75.8 0.8 dynamic-slice_negate_fusion
  76.5 17.4 %all-to-all-done.1 = f32[48,8,128]{2,1,0:T(8,128)S(1)} async-done(((f32[48,8,128]{2,1,0:T(8,128)}), f32[48,8,128]{2,1,0:T(8,128)S(1)}, u32[]{:S(2)}, u32[]{:S(2)}) %all-to-all-start.1) | async-done | bytes 196640 | tf_op jit(solution)/shard_map/all_to_all | solution.py:171
  94.0 0.1 multiply_convert_fusion
  94.1 0.1 broadcast_in_dim.2
  94.2 21.0 %all_to_all.16 = bf16[16,128,128]{2,1,0:T(8,128)(2,1)S(1)} all-to-all(bf16[16,128,128]{2,1,0:T(8,128)(2,1)S(1)} %broadcast_in_dim.2), channel_id=1, replica_groups=mesh['y_lo'=4,'z_hi'=3,'z_lo'=4,'x'=4,'y_hi'=2,'core'=2] {'y_lo','z_lo'}, dimensions={0} | all-to-all | bytes 1048576 | tf_op jit(solution)/shard_map/all_to_all | solution.py:171
  115.2 1.1 bitcast_convert_fusion
  (2 shorter events, 0.0 us)
Async XLA Ops:
  3.7 50.5 %copy-start = (bf16[2,544,256]{2,1,0:T(8,128)(2,1)S(1)}, bf16[2,544,256]{2,1,0:T(8,128)(2,1)}, u32[]{:S(2)}) copy-start(bf16[2,544,256]{2,1,0:T(8,128)(2,1)} %constant.44.clone.outer_ref) | copy-start | bytes 1671172
  3.7 50.5 %copy-start.1 = (bf16[2,256,256]{2,1,0:T(8,128)(2,1)S(1)}, bf16[2,256,256]{2,1,0:T(8,128)(2,1)}, u32[]{:S(2)}) copy-start(bf16[2,256,256]{2,1,0:T(8,128)(2,1)} %constant.45.clone.fwd_ref) | copy-start | bytes 786436
  3.7 50.5 %copy-start.2 = (bf16[2,256,256]{2,1,0:T(8,128)(2,1)S(1)}, bf16[2,256,256]{2,1,0:T(8,128)(2,1)}, u32[]{:S(2)}) copy-start(bf16[2,256,256]{2,1,0:T(8,128)(2,1)} %constant.46.clone.bwd_ref) | copy-start | bytes 786436
  3.7 50.5 %copy-start.3 = (f32[18,2,8,128]{3,2,1,0:T(8,128)S(1)}, f32[18,2,8,128]{3,2,1,0:T(8,128)}, u32[]{:S(2)}) copy-start(f32[18,2,8,128]{3,2,1,0:T(8,128)} %constant.47.clone.twist_ref) | copy-start | bytes 442372
  61.2 32.8 %all-to-all-start.1 = ((f32[48,8,128]{2,1,0:T(8,128)}), f32[48,8,128]{2,1,0:T(8,128)S(1)}, u32[]{:S(2)}, u32[]{:S(2)}) async-start(f32[48,8,128]{2,1,0:T(8,128)} %bitcast.1), calls=%async_computation.1 | async-start | bytes 393216 | tf_op jit(solution)/shard_map/all_to_all | solution.py:171

commit v2 on v1

--- a/solution.py
+++ b/solution.py
@@ -73,7 +73,7 @@
 
 def gate(q_gate, k_gate, values, out_grad):
     chans = q_gate.shape[1]
-    tile = min(chans, 512)
+    tile = min(chans, 1024)
     spec = pl.BlockSpec((1, tile, SPAN), lambda i: (0, i, 0))
     return pl.pallas_call(
         gate_kernel,
@@ -87,29 +87,30 @@
 
 def correlate_kernel(x_ref, outer_ref, fwd_ref, bwd_ref, twist_ref, out_ref, high_ref, low_ref):
     seqs = x_ref.shape[0]
-    copies = out_ref.shape[0]
     cos = twist_ref[:, 0]
     sin = twist_ref[:, 1]
 
     def outer_step(s, carry):
-        x = x_ref[s].reshape(BLOCKS * ROWS, SPAN)
-        y = dot(outer_ref[0], x) + dot(outer_ref[1], x)
-        y = y.reshape(FREQS, 2, 2, CHANS, SPAN)
-        real, imag = y[:, 0], y[:, 1]
+        x = x_ref[pl.ds(2 * s, 2)].reshape(2, BLOCKS * ROWS, SPAN)
+        x = jnp.concatenate([x[0], x[1]], axis=1)
+        y2 = dot(outer_ref[0], x) + dot(outer_ref[1], x)
         c = cos[:FREQS, None]
         d = sin[:FREQS, None]
-        turned_real = (real * c + imag * d).reshape(FREQS, ROWS, SPAN)
-        turned_imag = (imag * c - real * d).reshape(FREQS, ROWS, SPAN)
-        rows = pl.ds(pl.multiple_of(s * ROWS, ROWS), ROWS)
-        high, low = halves(turned_real)
-        high_ref[:, rows, :SPAN] = high
-        low_ref[:, rows, :SPAN] = low
-        high, low = halves(turned_imag)
-        high_ref[:, rows, SPAN:] = high
-        low_ref[:, rows, SPAN:] = low
+        for h in range(2):
+            y = y2[:, h * SPAN : (h + 1) * SPAN].reshape(FREQS, 2, 2, CHANS, SPAN)
+            real, imag = y[:, 0], y[:, 1]
+            turned_real = (real * c + imag * d).reshape(FREQS, ROWS, SPAN)
+            turned_imag = (imag * c - real * d).reshape(FREQS, ROWS, SPAN)
+            rows = pl.ds(pl.multiple_of((2 * s + h) * ROWS, ROWS), ROWS)
+            high, low = halves(turned_real)
+            high_ref[:, rows, :SPAN] = high
+            low_ref[:, rows, :SPAN] = low
+            high, low = halves(turned_imag)
+            high_ref[:, rows, SPAN:] = high
+            low_ref[:, rows, SPAN:] = low
         return carry
 
-    lax.fori_loop(0, seqs, outer_step, 0, unroll=2 if seqs % 2 == 0 else 1)
+    lax.fori_loop(0, seqs // 2, outer_step, 0, unroll=True)
 
     cross = []
     for k in range(FREQS):
@@ -139,11 +140,10 @@
             if k * n % BLOCKS:
                 term = term - turned_imag[k] * (weight * math.sin(angle))
             total = term if total is None else total + term
-        for copy in range(copies):
-            out_ref[copy, n] = total
-
-
-def correlate(x, copies):
+        out_ref[n] = total.astype(BF16)
+
+
+def correlate(x):
     seqs = x.shape[0]
     outer, forward, backward, twist = tables()
     rows = seqs * ROWS
@@ -152,7 +152,7 @@
         correlate_kernel,
         in_specs=[pl.BlockSpec(memory_space=pltpu.VMEM)] * 5,
         out_specs=pl.BlockSpec(memory_space=pltpu.VMEM),
-        out_shape=jax.ShapeDtypeStruct((copies, BLOCKS, CHANS, SPAN), F32),
+        out_shape=jax.ShapeDtypeStruct((BLOCKS, CHANS, SPAN), BF16),
         scratch_shapes=[
             pltpu.VMEM((FREQS, rows, 2 * SPAN), BF16),
             pltpu.VMEM((FREQS, rows, 2 * SPAN), BF16),
@@ -171,23 +171,37 @@
     return lax.all_to_all(x, axes, split_axis=0, concat_axis=0, tiled=True)
 
 
+def sum_far(part):
+    far = lax.axis_size("z_hi")
+    here = lax.axis_index("z_hi")
+    held = [part]
+    for step in range(1, far):
+        held.append(lax.ppermute(part, "z_hi", [(i, (i + step) % far) for i in range(far)]))
+    held = [x.astype(F32) for x in held]
+    total = None
+    for place in range(far):
+        term = held[0]
+        for step in range(1, far):
+            term = jnp.where((here - place) % far == step, held[step], term)
+        total = term if total is None else total + term
+    return total
+
+
 def body(length, batch, q_gate, k_gate, values, out_grad, decay):
     near = lax.axis_size(NEAR)
-    far = lax.axis_size("z_hi")
     gated = gate(q_gate, k_gate, values, out_grad)
     whole = to_each(gated, NEAR + CTX)
-    part = correlate(whole.reshape(near, BLOCKS, ROWS, SPAN), far)
-
-    group = BLOCKS * CHANS
-    mine = lax.dynamic_slice_in_dim(decay, lax.axis_index(NEAR) * group, group)
-    lags = (lax.axis_index(CTX) * SPAN + jnp.arange(SPAN, dtype=jnp.int32)).astype(F32)
-    window = jnp.exp(-mine[:, None] * lags[None, :] / length) / math.sqrt(batch * length)
-
-    sent = part.reshape(far * BLOCKS, CHANS, SPAN)
-    lag_parts = to_each(sent, ("z_hi",) + CTX).reshape(far, group, SPAN)
-    ours = (jnp.sum(lag_parts, axis=0) * window).astype(BF16)
-    everyone = to_each(jnp.broadcast_to(ours[None], (near, group, SPAN)), NEAR)
-    return everyone.reshape(near * group, SPAN).astype(F32)
+    part = correlate(whole.reshape(near, BLOCKS, ROWS, SPAN))
+
+    first = (lax.axis_index(NEAR) * BLOCKS + lax.axis_index(CTX)) * CHANS
+    mine = lax.dynamic_slice_in_dim(decay, first, CHANS)
+    lags = jnp.arange(length, dtype=jnp.int32).astype(F32).reshape(BLOCKS, 1, SPAN)
+    window = jnp.exp(-mine[None, :, None] * lags / length) / math.sqrt(batch * length)
+    ours = (sum_far(part) * window).astype(BF16)
+
+    sent = jnp.broadcast_to(ours[None], (near, BLOCKS, CHANS, SPAN))
+    everyone = to_each(sent.reshape(near * BLOCKS, CHANS, SPAN), NEAR + CTX)
+    return everyone.reshape(near * BLOCKS * CHANS, SPAN).astype(F32)
 
 
 def solution(mesh):

time: 117 us -> 109 us (0.932)
  blocking collectives: 71.6 us -> 29.9 us
  waiting for transfers between devices: 17.4 us -> 37.5 us
  starting transfers between devices: 14.5 us -> 33 us
  Pallas kernels: 10.6 us -> 5.92 us
    all_to_all x2 -> x1, blocking collectives: 71.6 us -> 29.9 us  [to_each(): return lax.all_to_all(x, axes, split_axis=0, concat_axis=0, tiled=True)]
    all_to_all x1, waiting for transfers between devices: 17.4 us -> 31 us  [to_each(): return lax.all_to_all(x, axes, split_axis=0, concat_axis=0, tiled=True)]
    ppermute x0 -> x2, starting transfers between devices: none -> 13.5 us  [sum_far(): lax.ppermute(part, 'z_hi', [(i, (i + step) % far) for i in range(far)])]
    ppermute x0 -> x2, waiting for transfers between devices: none -> 6.47 us  [sum_far(): lax.ppermute(part, 'z_hi', [(i, (i + step) % far) for i in range(far)])]
    all_to_all x1, starting transfers between devices: 14.5 us -> 19.5 us  [to_each(): return lax.all_to_all(x, axes, split_axis=0, concat_axis=0, tiled=True)]
    pallas_call x1, Pallas kernels: 6.94 us -> 3.49 us  [correlate(): pl.pallas_call(correlate_kernel, in_specs=[pl.BlockSpec(memory_space=pltp...]
    pallas_call x1, Pallas kernels: 3.69 us -> 2.42 us  [gate(): pl.pallas_call(gate_kernel, grid=(chans // tile,), in_specs=[spec] * 4, o...]
  transfers between devices with their start and end apart: 1 -> 3, of which waited for: 1 -> 2; matrix products, arithmetic and copies ran while one was open for 1% -> 1% of each run, Pallas kernels for 0% -> 0%
where the time goes in v2:
time: 109 us; the launch traced here: 108 us
  waiting for transfers between devices  37.5 us (34%)
  starting transfers between devices  33 us (30%)
  blocking collectives  29.9 us (27%)
  Pallas kernels  5.92 us (5%)
  other arithmetic  1.9 us (2%)
    all_to_all x1, waiting for transfers between devices, to_each(): return lax.all_to_all(x, axes, split_axis=0, concat_axis=0, tiled=True)  31 us
    all_to_all x1, blocking collectives, to_each(): return lax.all_to_all(x, axes, split_axis=0, concat_axis=0, tiled=True)  29.9 us
    all_to_all x1, starting transfers between devices, to_each(): return lax.all_to_all(x, axes, split_axis=0, concat_axis=0, tiled=True)  19.5 us
    ppermute x2, starting transfers between devices, sum_far(): lax.ppermute(part, 'z_hi', [(i, (i + step) % far) for i in range(far)])  13.5 us
    ppermute x2, waiting for transfers between devices, sum_far(): lax.ppermute(part, 'z_hi', [(i, (i + step) % far) for i in range(far)])  6.47 us
    pallas_call x1, Pallas kernels, correlate(): pl.pallas_call(correlate_kernel, in_specs=[pl.BlockSpec(memory_space=pltp...  3.49 us
    pallas_call x1, Pallas kernels, gate(): pl.pallas_call(gate_kernel, grid=(chans // tile,), in_specs=[spec] * 4, o...  2.42 us
  transfers between devices with their start and end apart: 3, of which 2 were waited for; matrix products, arithmetic and copies ran while one was open for 1% of the time, Pallas kernels for 0%

profile of v2, /device:TPU:1, one launch (start us, length us, event | category | flops | bytes accessed | tf_op | source)
XLA Modules:
  0.0 108.4 jit_solution(5247750943472299237)
XLA Ops:
  0.0 2.4 %gate.1 = bf16[256,16,128]{2,1,0:T(8,128)(2,1)} custom-call(bf16[1,2048,128]{2,1,0:T(8,128)(2,1)} %k_ref.1, bf16[1,2048,128]{2,1,0:T(8,128)(2,1)} %v_ref.1, bf16[1,2048,128]{2,1,0:T(8,128)(2,1)} %q_ref.1, bf16[1,2048,128]{2,1,0:T(8,128)(2,1)} %g_ref.1), custom_call_target="tpu_custom_call" | custom-call | tf_op jit(solution)/shard_map/gate/pallas_call | solution.py:78
  2.4 0.0 copy-start
  2.4 0.0 copy-start.1
  2.4 0.0 copy-start.2
  2.4 0.0 copy-start.3
  2.5 19.5 %all-to-all-start = ((bf16[256,16,128]{2,1,0:T(8,128)(2,1)}), bf16[256,16,128]{2,1,0:T(8,128)(2,1)S(1)}, u32[]{:S(2)}, u32[]{:S(2)}) async-start(bf16[256,16,128]{2,1,0:T(8,128)(2,1)} %gate.1), calls=%async_computation | async-start | bytes 2097152 | tf_op jit(solution)/shard_map/all_to_all | solution.py:171
  22.0 31.0 %all-to-all-done = bf16[256,16,128]{2,1,0:T(8,128)(2,1)S(1)} async-done(((bf16[256,16,128]{2,1,0:T(8,128)(2,1)}), bf16[256,16,128]{2,1,0:T(8,128)(2,1)S(1)}, u32[]{:S(2)}, u32[]{:S(2)}) %all-to-all-start) | async-done | bytes 1048608 | tf_op jit(solution)/shard_map/all_to_all | solution.py:171
  53.0 0.0 copy-done
  53.0 0.0 copy-done.1
  53.0 0.0 copy-done.2
  53.0 0.0 copy-done.3
  53.0 3.5 %correlate.1 = bf16[16,8,128]{2,1,0:T(8,128)(2,1)S(1)} custom-call(bf16[16,16,16,128]{3,2,1,0:T(8,128)(2,1)S(1)} %bitcast.5, bf16[2,544,256]{2,1,0:T(8,128)(2,1)S(1)} %copy-done, bf16[2,256,256]{2,1,0:T(8,128)(2,1)S(1)} %copy-done.1, bf16[2,256,256]{2,1,0:T(8,128)(2,1)S(1)} %copy-done.2, f32[18,2,8,128]{3,2,1,0:T(8,128)S(1)} %copy-done.3), custom_call_target="tpu_custom_call" | custom-call | flops 2852126720 | bytes 3000000 | tf_op jit(solution)/shard_map/correlate/pallas_call | solution.py:151
  56.5 11.6 %collective-permute-start = (bf16[16,8,128]{2,1,0:T(8,128)(2,1)S(1)}, bf16[16,8,128]{2,1,0:T(8,128)(2,1)S(1)}, u32[]{:S(2)}, u32[]{:S(2)}) collective-permute-start(bf16[16,8,128]{2,1,0:T(8,128)(2,1)S(1)} %correlate.1), channel_id=1, source_target_pairs={{0,128},{64,0},{128,64},{1,129},{65,1},{129,65},{2,130},{66,2},{13... | collective-permute-start | bytes 98312 | tf_op jit(solution)/shard_map/ppermute | solution.py:179
  68.1 1.9 %collective-permute-start.1 = (bf16[16,8,128]{2,1,0:T(8,128)(2,1)S(1)}, bf16[16,8,128]{2,1,0:T(8,128)(2,1)S(1)}, u32[]{:S(2)}, u32[]{:S(2)}) collective-permute-start(bf16[16,8,128]{2,1,0:T(8,128)(2,1)S(1)} %correlate.1), channel_id=1, source_target_pairs={{0,64},{64,128},{128,0},{1,65},{65,129},{129,1},{2,66},{66,130},{1... | collective-permute-start | bytes 98312 | tf_op jit(solution)/shard_map/ppermute | solution.py:179
  70.0 0.8 dynamic-slice_negate_fusion
  70.8 0.0 collective-permute-done
  70.8 6.5 %collective-permute-done.1 = bf16[16,8,128]{2,1,0:T(8,128)(2,1)S(1)} collective-permute-done((bf16[16,8,128]{2,1,0:T(8,128)(2,1)S(1)}, bf16[16,8,128]{2,1,0:T(8,128)(2,1)S(1)}, u32[]{:S(2)}, u32[]{:S(2)}) %collective-permute-start.1) | collective-permute-done | bytes 32800 | tf_op jit(solution)/shard_map/ppermute | solution.py:179
  77.2 0.1 fusion.3
  77.3 0.1 broadcast_in_dim.2
  77.4 29.9 %all_to_all.10 = bf16[256,8,128]{2,1,0:T(8,128)(2,1)S(1)} all-to-all(bf16[256,8,128]{2,1,0:T(8,128)(2,1)S(1)} %bitcast.6), channel_id=1, replica_groups=mesh['y_lo'=4,'z_hi'=3,'z_lo'=4,'x'=4,'y_hi'=2,'core'=2] {'y_lo','z_lo',..., dimensions={0} | all-to-all | bytes 1048576 | tf_op jit(solution)/shard_map/all_to_all | solution.py:171
  107.4 1.0 bitcast_convert_fusion
  (1 shorter events, 0.0 us)
Async XLA Ops:
  2.4 50.5 %copy-start = (bf16[2,544,256]{2,1,0:T(8,128)(2,1)S(1)}, bf16[2,544,256]{2,1,0:T(8,128)(2,1)}, u32[]{:S(2)}) copy-start(bf16[2,544,256]{2,1,0:T(8,128)(2,1)} %constant.77.clone.outer_ref) | copy-start | bytes 1671172
  2.4 50.6 %copy-start.1 = (bf16[2,256,256]{2,1,0:T(8,128)(2,1)S(1)}, bf16[2,256,256]{2,1,0:T(8,128)(2,1)}, u32[]{:S(2)}) copy-start(bf16[2,256,256]{2,1,0:T(8,128)(2,1)} %constant.78.clone.fwd_ref) | copy-start | bytes 786436
  2.4 50.6 %copy-start.2 = (bf16[2,256,256]{2,1,0:T(8,128)(2,1)S(1)}, bf16[2,256,256]{2,1,0:T(8,128)(2,1)}, u32[]{:S(2)}) copy-start(bf16[2,256,256]{2,1,0:T(8,128)(2,1)} %constant.79.clone.bwd_ref) | copy-start | bytes 786436
  2.4 50.5 %copy-start.3 = (f32[18,2,8,128]{3,2,1,0:T(8,128)S(1)}, f32[18,2,8,128]{3,2,1,0:T(8,128)}, u32[]{:S(2)}) copy-start(f32[18,2,8,128]{3,2,1,0:T(8,128)} %constant.80.clone.twist_ref) | copy-start | bytes 442372
  2.5 50.5 %all-to-all-start = ((bf16[256,16,128]{2,1,0:T(8,128)(2,1)}), bf16[256,16,128]{2,1,0:T(8,128)(2,1)S(1)}, u32[]{:S(2)}, u32[]{:S(2)}) async-start(bf16[256,16,128]{2,1,0:T(8,128)(2,1)} %gate.1), calls=%async_computation | async-start | bytes 2097152 | tf_op jit(solution)/shard_map/all_to_all | solution.py:171
  56.5 14.3 %collective-permute-start = (bf16[16,8,128]{2,1,0:T(8,128)(2,1)S(1)}, bf16[16,8,128]{2,1,0:T(8,128)(2,1)S(1)}, u32[]{:S(2)}, u32[]{:S(2)}) collective-permute-start(bf16[16,8,128]{2,1,0:T(8,128)(2,1)S(1)} %correlate.1), channel_id=1, source_target_pairs={{0,128},{64,0},{128,64},{1,129},{65,1},{129,65},{2,130},{66,2},{13... | collective-permute-start | bytes 98312 | tf_op jit(solution)/shard_map/ppermute | solution.py:179
  68.1 9.2 %collective-permute-start.1 = (bf16[16,8,128]{2,1,0:T(8,128)(2,1)S(1)}, bf16[16,8,128]{2,1,0:T(8,128)(2,1)S(1)}, u32[]{:S(2)}, u32[]{:S(2)}) collective-permute-start(bf16[16,8,128]{2,1,0:T(8,128)(2,1)S(1)} %correlate.1), channel_id=1, source_target_pairs={{0,64},{64,128},{128,0},{1,65},{65,129},{129,1},{2,66},{66,130},{1... | collective-permute-start | bytes 98312 | tf_op jit(solution)/shard_map/ppermute | solution.py:179

commit v3 on v2

--- a/solution.py
+++ b/solution.py
@@ -171,22 +171,6 @@
     return lax.all_to_all(x, axes, split_axis=0, concat_axis=0, tiled=True)
 
 
-def sum_far(part):
-    far = lax.axis_size("z_hi")
-    here = lax.axis_index("z_hi")
-    held = [part]
-    for step in range(1, far):
-        held.append(lax.ppermute(part, "z_hi", [(i, (i + step) % far) for i in range(far)]))
-    held = [x.astype(F32) for x in held]
-    total = None
-    for place in range(far):
-        term = held[0]
-        for step in range(1, far):
-            term = jnp.where((here - place) % far == step, held[step], term)
-        total = term if total is None else total + term
-    return total
-
-
 def body(length, batch, q_gate, k_gate, values, out_grad, decay):
     near = lax.axis_size(NEAR)
     gated = gate(q_gate, k_gate, values, out_grad)
@@ -197,7 +181,8 @@
     mine = lax.dynamic_slice_in_dim(decay, first, CHANS)
     lags = jnp.arange(length, dtype=jnp.int32).astype(F32).reshape(BLOCKS, 1, SPAN)
     window = jnp.exp(-mine[None, :, None] * lags / length) / math.sqrt(batch * length)
-    ours = (sum_far(part) * window).astype(BF16)
+    parts = lax.all_gather(part, "z_hi", axis=0)
+    ours = (jnp.sum(parts.astype(F32), axis=0) * window).astype(BF16)
 
     sent = jnp.broadcast_to(ours[None], (near, BLOCKS, CHANS, SPAN))
     everyone = to_each(sent.reshape(near * BLOCKS, CHANS, SPAN), NEAR + CTX)

time: 109 us -> 107 us (0.982)
  blocking collectives: 29.9 us -> 48.5 us
  starting transfers between devices: 33 us -> 19.5 us
  waiting for transfers between devices: 37.5 us -> 30.2 us
    all_gather x0 -> x1, blocking collectives: none -> 19.1 us  [body(): parts = lax.all_gather(part, 'z_hi', axis=0)]
    ppermute x2 -> x0, starting transfers between devices: 13.5 us -> none  [sum_far(): lax.ppermute(part, 'z_hi', [(i, (i + step) % far) for i in range(far)])]
    ppermute x2 -> x0, waiting for transfers between devices: 6.47 us -> none  [sum_far(): lax.ppermute(part, 'z_hi', [(i, (i + step) % far) for i in range(far)])]
  transfers between devices with their start and end apart: 3 -> 1, of which waited for: 2 -> 1; matrix products, arithmetic and copies ran while one was open for 1% -> 1% of each run, Pallas kernels for 0% -> 0%
where the time goes in v3:
time: 107 us; the launch traced here: 106 us
  blocking collectives  48.5 us (45%)
  waiting for transfers between devices  30.2 us (28%)
  starting transfers between devices  19.5 us (18%)
  Pallas kernels  5.92 us (6%)
  other arithmetic  1.92 us (2%)
    all_to_all x1, waiting for transfers between devices, to_each(): return lax.all_to_all(x, axes, split_axis=0, concat_axis=0, tiled=True)  30.2 us
    all_to_all x1, blocking collectives, to_each(): return lax.all_to_all(x, axes, split_axis=0, concat_axis=0, tiled=True)  29.4 us
    all_to_all x1, starting transfers between devices, to_each(): return lax.all_to_all(x, axes, split_axis=0, concat_axis=0, tiled=True)  19.5 us
    all_gather x1, blocking collectives, body(): parts = lax.all_gather(part, 'z_hi', axis=0)  19.1 us
    pallas_call x1, Pallas kernels, correlate(): pl.pallas_call(correlate_kernel, in_specs=[pl.BlockSpec(memory_space=pltp...  3.49 us
    pallas_call x1, Pallas kernels, gate(): pl.pallas_call(gate_kernel, grid=(chans // tile,), in_specs=[spec] * 4, o...  2.42 us
  transfers between devices with their start and end apart: 1, of which 1 were waited for; matrix products, arithmetic and copies ran while one was open for 1% of the time, Pallas kernels for 0%

profile of v3, /device:TPU:1, one launch (start us, length us, event | category | flops | bytes accessed | tf_op | source)
XLA Modules:
  0.0 106.3 jit_solution(5958828663526753114)
XLA Ops:
  0.0 2.4 %gate.1 = bf16[256,16,128]{2,1,0:T(8,128)(2,1)} custom-call(bf16[1,2048,128]{2,1,0:T(8,128)(2,1)} %k_ref.1, bf16[1,2048,128]{2,1,0:T(8,128)(2,1)} %v_ref.1, bf16[1,2048,128]{2,1,0:T(8,128)(2,1)} %q_ref.1, bf16[1,2048,128]{2,1,0:T(8,128)(2,1)} %g_ref.1), custom_call_target="tpu_custom_call" | custom-call | tf_op jit(solution)/shard_map/gate/pallas_call | solution.py:78
  2.4 0.0 copy-start
  2.4 0.0 copy-start.1
  2.4 0.0 copy-start.2
  2.4 0.0 copy-start.3
  2.5 19.5 %all-to-all-start = ((bf16[256,16,128]{2,1,0:T(8,128)(2,1)}), bf16[256,16,128]{2,1,0:T(8,128)(2,1)S(1)}, u32[]{:S(2)}, u32[]{:S(2)}) async-start(bf16[256,16,128]{2,1,0:T(8,128)(2,1)} %gate.1), calls=%async_computation | async-start | bytes 2097152 | tf_op jit(solution)/shard_map/all_to_all | solution.py:171
  22.0 0.8 dynamic-slice_negate_fusion
  22.7 30.2 %all-to-all-done = bf16[256,16,128]{2,1,0:T(8,128)(2,1)S(1)} async-done(((bf16[256,16,128]{2,1,0:T(8,128)(2,1)}), bf16[256,16,128]{2,1,0:T(8,128)(2,1)S(1)}, u32[]{:S(2)}, u32[]{:S(2)}) %all-to-all-start) | async-done | bytes 1048608 | tf_op jit(solution)/shard_map/all_to_all | solution.py:171
  53.0 0.0 copy-done
  53.0 0.0 copy-done.1
  53.0 0.0 copy-done.2
  53.0 0.0 copy-done.3
  53.0 3.5 %correlate.1 = bf16[16,8,128]{2,1,0:T(8,128)(2,1)S(1)} custom-call(bf16[16,16,16,128]{3,2,1,0:T(8,128)(2,1)S(1)} %bitcast.7, bf16[2,544,256]{2,1,0:T(8,128)(2,1)S(1)} %copy-done, bf16[2,256,256]{2,1,0:T(8,128)(2,1)S(1)} %copy-done.1, bf16[2,256,256]{2,1,0:T(8,128)(2,1)S(1)} %copy-done.2, f32[18,2,8,128]{3,2,1,0:T(8,128)S(1)} %copy-done.3), custom_call_target="tpu_custom_call" | custom-call | flops 2852126720 | bytes 3000000 | tf_op jit(solution)/shard_map/correlate/pallas_call | solution.py:151
  56.5 19.1 %all-gather = bf16[48,8,128]{2,1,0:T(8,128)(2,1)S(1)} all-gather(bf16[16,8,128]{2,1,0:T(8,128)(2,1)S(1)} %correlate.1), channel_id=2, replica_groups=mesh['y_lo'=4,'z_hi'=3,'z_lo'=4,'x'=4,'y_hi'=2,'core'=2] {'z_hi'}, dimensions={0}, use_global_device_ids=true | all-gather | bytes 131072 | tf_op jit(solution)/shard_map/all_gather | solution.py:184
  75.6 0.1 multiply_convert_fusion
  75.7 0.1 broadcast_in_dim.2
  75.8 29.4 %all_to_all.10 = bf16[256,8,128]{2,1,0:T(8,128)(2,1)S(1)} all-to-all(bf16[256,8,128]{2,1,0:T(8,128)(2,1)S(1)} %bitcast.8), channel_id=1, replica_groups=mesh['y_lo'=4,'z_hi'=3,'z_lo'=4,'x'=4,'y_hi'=2,'core'=2] {'y_lo','z_lo',..., dimensions={0} | all-to-all | bytes 1048576 | tf_op jit(solution)/shard_map/all_to_all | solution.py:171
  105.3 1.0 bitcast_convert_fusion
  (2 shorter events, 0.0 us)
Async XLA Ops:
  2.4 50.5 %copy-start = (bf16[2,544,256]{2,1,0:T(8,128)(2,1)S(1)}, bf16[2,544,256]{2,1,0:T(8,128)(2,1)}, u32[]{:S(2)}) copy-start(bf16[2,544,256]{2,1,0:T(8,128)(2,1)} %constant.50.clone.outer_ref) | copy-start | bytes 1671172
  2.4 50.6 %copy-start.1 = (bf16[2,256,256]{2,1,0:T(8,128)(2,1)S(1)}, bf16[2,256,256]{2,1,0:T(8,128)(2,1)}, u32[]{:S(2)}) copy-start(bf16[2,256,256]{2,1,0:T(8,128)(2,1)} %constant.51.clone.fwd_ref) | copy-start | bytes 786436
  2.4 50.6 %copy-start.2 = (bf16[2,256,256]{2,1,0:T(8,128)(2,1)S(1)}, bf16[2,256,256]{2,1,0:T(8,128)(2,1)}, u32[]{:S(2)}) copy-start(bf16[2,256,256]{2,1,0:T(8,128)(2,1)} %constant.52.clone.bwd_ref) | copy-start | bytes 786436
  2.4 50.5 %copy-start.3 = (f32[18,2,8,128]{3,2,1,0:T(8,128)S(1)}, f32[18,2,8,128]{3,2,1,0:T(8,128)}, u32[]{:S(2)}) copy-start(f32[18,2,8,128]{3,2,1,0:T(8,128)} %constant.53.clone.twist_ref) | copy-start | bytes 442372
  2.5 50.5 %all-to-all-start = ((bf16[256,16,128]{2,1,0:T(8,128)(2,1)}), bf16[256,16,128]{2,1,0:T(8,128)(2,1)S(1)}, u32[]{:S(2)}, u32[]{:S(2)}) async-start(bf16[256,16,128]{2,1,0:T(8,128)(2,1)} %gate.1), calls=%async_computation | async-start | bytes 2097152 | tf_op jit(solution)/shard_map/all_to_all | solution.py:171

commit v4 on v3

--- a/solution.py
+++ b/solution.py
@@ -87,6 +87,7 @@
 
 def correlate_kernel(x_ref, outer_ref, fwd_ref, bwd_ref, twist_ref, out_ref, high_ref, low_ref):
     seqs = x_ref.shape[0]
+    copies = out_ref.shape[0]
     cos = twist_ref[:, 0]
     sin = twist_ref[:, 1]
 
@@ -140,10 +141,11 @@
             if k * n % BLOCKS:
                 term = term - turned_imag[k] * (weight * math.sin(angle))
             total = term if total is None else total + term
-        out_ref[n] = total.astype(BF16)
-
-
-def correlate(x):
+        for copy in range(copies):
+            out_ref[copy, n] = total.astype(BF16)
+
+
+def correlate(x, copies):
     seqs = x.shape[0]
     outer, forward, backward, twist = tables()
     rows = seqs * ROWS
@@ -152,7 +154,7 @@
         correlate_kernel,
         in_specs=[pl.BlockSpec(memory_space=pltpu.VMEM)] * 5,
         out_specs=pl.BlockSpec(memory_space=pltpu.VMEM),
-        out_shape=jax.ShapeDtypeStruct((BLOCKS, CHANS, SPAN), BF16),
+        out_shape=jax.ShapeDtypeStruct((copies, BLOCKS, CHANS, SPAN), BF16),
         scratch_shapes=[
             pltpu.VMEM((FREQS, rows, 2 * SPAN), BF16),
             pltpu.VMEM((FREQS, rows, 2 * SPAN), BF16),
@@ -175,13 +177,15 @@
     near = lax.axis_size(NEAR)
     gated = gate(q_gate, k_gate, values, out_grad)
     whole = to_each(gated, NEAR + CTX)
-    part = correlate(whole.reshape(near, BLOCKS, ROWS, SPAN))
 
     first = (lax.axis_index(NEAR) * BLOCKS + lax.axis_index(CTX)) * CHANS
     mine = lax.dynamic_slice_in_dim(decay, first, CHANS)
     lags = jnp.arange(length, dtype=jnp.int32).astype(F32).reshape(BLOCKS, 1, SPAN)
     window = jnp.exp(-mine[None, :, None] * lags / length) / math.sqrt(batch * length)
-    parts = lax.all_gather(part, "z_hi", axis=0)
+    whole, window = lax.optimization_barrier((whole, window))
+
+    part = correlate(whole.reshape(near, BLOCKS, ROWS, SPAN), lax.axis_size("z_hi"))
+    parts = to_each(part, "z_hi")
     ours = (jnp.sum(parts.astype(F32), axis=0) * window).astype(BF16)
 
     sent = jnp.broadcast_to(ours[None], (near, BLOCKS, CHANS, SPAN))

time: 107 us -> 106 us (level)
    all_gather x1 -> x0, blocking collectives: 19.1 us -> none  [body(): parts = lax.all_gather(part, 'z_hi', axis=0)]
    all_to_all x1 -> x2, blocking collectives: 29.4 us -> 48.3 us  [to_each(): return lax.all_to_all(x, axes, split_axis=0, concat_axis=0, tiled=True)]
where the time goes in v4:
time: 106 us
  blocking collectives  48.3 us (46%)
  waiting for transfers between devices  30.2 us (28%)
  starting transfers between devices  19.5 us (18%)
  Pallas kernels  5.93 us (6%)
  other arithmetic  1.93 us (2%)
    all_to_all x2, blocking collectives, to_each(): return lax.all_to_all(x, axes, split_axis=0, concat_axis=0, tiled=True)  48.3 us
    all_to_all x1, waiting for transfers between devices, to_each(): return lax.all_to_all(x, axes, split_axis=0, concat_axis=0, tiled=True)  30.2 us
    all_to_all x1, starting transfers between devices, to_each(): return lax.all_to_all(x, axes, split_axis=0, concat_axis=0, tiled=True)  19.5 us
    pallas_call x1, Pallas kernels, correlate(): pl.pallas_call(correlate_kernel, in_specs=[pl.BlockSpec(memory_space=pltp...  3.5 us
    pallas_call x1, Pallas kernels, gate(): pl.pallas_call(gate_kernel, grid=(chans // tile,), in_specs=[spec] * 4, o...  2.42 us
  transfers between devices with their start and end apart: 1, of which 1 were waited for; matrix products, arithmetic and copies ran while one was open for 1% of the time, Pallas kernels for 0%

profile of v4, /device:TPU:1, one launch (start us, length us, event | category | flops | bytes accessed | tf_op | source)
XLA Modules:
  0.0 106.0 jit_solution(14674946365333715508)
XLA Ops:
  0.0 2.4 %gate.1 = bf16[256,16,128]{2,1,0:T(8,128)(2,1)} custom-call(bf16[1,2048,128]{2,1,0:T(8,128)(2,1)} %k_ref.1, bf16[1,2048,128]{2,1,0:T(8,128)(2,1)} %v_ref.1, bf16[1,2048,128]{2,1,0:T(8,128)(2,1)} %q_ref.1, bf16[1,2048,128]{2,1,0:T(8,128)(2,1)} %g_ref.1), custom_call_target="tpu_custom_call" | custom-call | tf_op jit(solution)/shard_map/gate/pallas_call | solution.py:78
  2.4 0.0 copy-start
  2.4 0.0 copy-start.1
  2.4 0.0 copy-start.2
  2.4 0.0 copy-start.3
  2.5 19.5 %all-to-all-start = ((bf16[256,16,128]{2,1,0:T(8,128)(2,1)}), bf16[256,16,128]{2,1,0:T(8,128)(2,1)S(1)}, u32[]{:S(2)}, u32[]{:S(2)}) async-start(bf16[256,16,128]{2,1,0:T(8,128)(2,1)} %gate.1), calls=%async_computation | async-start | bytes 2097152 | tf_op jit(solution)/shard_map/all_to_all | solution.py:173
  22.0 0.8 dynamic-slice_negate_fusion
  22.7 0.1 exponential_multiply_fusion
  22.8 30.2 %all-to-all-done = bf16[256,16,128]{2,1,0:T(8,128)(2,1)S(1)} async-done(((bf16[256,16,128]{2,1,0:T(8,128)(2,1)}), bf16[256,16,128]{2,1,0:T(8,128)(2,1)S(1)}, u32[]{:S(2)}, u32[]{:S(2)}) %all-to-all-start) | async-done | bytes 1048608 | tf_op jit(solution)/shard_map/all_to_all | solution.py:173
  53.0 0.0 copy-done
  53.0 0.0 copy-done.1
  53.0 0.0 copy-done.2
  53.0 0.0 copy-done.3
  53.0 3.5 %correlate.1 = bf16[3,16,8,128]{3,2,1,0:T(8,128)(2,1)S(1)} custom-call(bf16[16,16,16,128]{3,2,1,0:T(8,128)(2,1)S(1)} %bitcast.5, bf16[2,544,256]{2,1,0:T(8,128)(2,1)S(1)} %copy-done, bf16[2,256,256]{2,1,0:T(8,128)(2,1)S(1)} %copy-done.1, bf16[2,256,256]{2,1,0:T(8,128)(2,1)S(1)} %copy-done.2, f32[18,2,8,128]{3,2,1,0:T(8,128)S(1)} %copy-done.3), custom_call_target="tpu_custom_call" | custom-call | flops 2852126720 | bytes 3000000 | tf_op jit(solution)/shard_map/correlate/pallas_call | solution.py:153
  56.5 19.9 %all_to_all.15 = bf16[3,16,8,128]{3,2,1,0:T(8,128)(2,1)S(1)} all-to-all(bf16[3,16,8,128]{3,2,1,0:T(8,128)(2,1)S(1)} %correlate.1), channel_id=1, replica_groups=mesh['y_lo'=4,'z_hi'=3,'z_lo'=4,'x'=4,'y_hi'=2,'core'=2] {'z_hi'}, dimensions={0} | all-to-all | bytes 196608 | tf_op jit(solution)/shard_map/all_to_all | solution.py:173
  76.5 0.1 broadcast_in_dim.2
  76.6 28.4 %all_to_all.16 = bf16[256,8,128]{2,1,0:T(8,128)(2,1)S(1)} all-to-all(bf16[256,8,128]{2,1,0:T(8,128)(2,1)S(1)} %bitcast.6), channel_id=1, replica_groups=mesh['y_lo'=4,'z_hi'=3,'z_lo'=4,'x'=4,'y_hi'=2,'core'=2] {'y_lo','z_lo',..., dimensions={0} | all-to-all | bytes 1048576 | tf_op jit(solution)/shard_map/all_to_all | solution.py:173
  104.9 1.0 bitcast_convert_fusion
  (3 shorter events, 0.0 us)
Async XLA Ops:
  2.4 50.5 %copy-start = (bf16[2,544,256]{2,1,0:T(8,128)(2,1)S(1)}, bf16[2,544,256]{2,1,0:T(8,128)(2,1)}, u32[]{:S(2)}) copy-start(bf16[2,544,256]{2,1,0:T(8,128)(2,1)} %constant.50.clone.outer_ref) | copy-start | bytes 1671172
  2.4 50.6 %copy-start.1 = (bf16[2,256,256]{2,1,0:T(8,128)(2,1)S(1)}, bf16[2,256,256]{2,1,0:T(8,128)(2,1)}, u32[]{:S(2)}) copy-start(bf16[2,256,256]{2,1,0:T(8,128)(2,1)} %constant.51.clone.fwd_ref) | copy-start | bytes 786436
  2.4 50.6 %copy-start.2 = (bf16[2,256,256]{2,1,0:T(8,128)(2,1)S(1)}, bf16[2,256,256]{2,1,0:T(8,128)(2,1)}, u32[]{:S(2)}) copy-start(bf16[2,256,256]{2,1,0:T(8,128)(2,1)} %constant.52.clone.bwd_ref) | copy-start | bytes 786436
  2.4 50.5 %copy-start.3 = (f32[18,2,8,128]{3,2,1,0:T(8,128)S(1)}, f32[18,2,8,128]{3,2,1,0:T(8,128)}, u32[]{:S(2)}) copy-start(f32[18,2,8,128]{3,2,1,0:T(8,128)} %constant.53.clone.twist_ref) | copy-start | bytes 442372
  2.5 50.5 %all-to-all-start = ((bf16[256,16,128]{2,1,0:T(8,128)(2,1)}), bf16[256,16,128]{2,1,0:T(8,128)(2,1)S(1)}, u32[]{:S(2)}, u32[]{:S(2)}) async-start(bf16[256,16,128]{2,1,0:T(8,128)(2,1)} %gate.1), calls=%async_computation | async-start | bytes 2097152 | tf_op jit(solution)/shard_map/all_to_all | solution.py:173

commit v5 on v4

--- a/solution.py
+++ b/solution.py
@@ -165,6 +165,26 @@
     )(x, outer, forward, backward, twist)
 
 
+def finish_kernel(parts_ref, window_ref, out_ref):
+    total = parts_ref[0].astype(F32)
+    for place in range(1, parts_ref.shape[0]):
+        total = total + parts_ref[place].astype(F32)
+    ours = (total * window_ref[...]).astype(BF16)
+    for copy in range(out_ref.shape[0]):
+        out_ref[copy] = ours
+
+
+def finish(parts, window, copies):
+    return pl.pallas_call(
+        finish_kernel,
+        in_specs=[pl.BlockSpec(memory_space=pltpu.VMEM)] * 2,
+        out_specs=pl.BlockSpec(memory_space=pltpu.VMEM),
+        out_shape=jax.ShapeDtypeStruct((copies,) + window.shape, BF16),
+        compiler_params=pltpu.CompilerParams(vmem_limit_bytes=16 * 1024 * 1024),
+        name="finish",
+    )(parts, window)
+
+
 CTX = ("x", "y_hi", "core")
 NEAR = ("y_lo", "z_lo")
 
@@ -186,9 +206,7 @@
 
     part = correlate(whole.reshape(near, BLOCKS, ROWS, SPAN), lax.axis_size("z_hi"))
     parts = to_each(part, "z_hi")
-    ours = (jnp.sum(parts.astype(F32), axis=0) * window).astype(BF16)
-
-    sent = jnp.broadcast_to(ours[None], (near, BLOCKS, CHANS, SPAN))
+    sent = finish(parts, window, near)
     everyone = to_each(sent.reshape(near * BLOCKS, CHANS, SPAN), NEAR + CTX)
     return everyone.reshape(near * BLOCKS * CHANS, SPAN).astype(F32)
 

time: 106 us -> 106 us (level)
  no operation moved by 1% of the time
where the time goes in v5:
time: 106 us
  blocking collectives  48.3 us (46%)
  waiting for transfers between devices  30.2 us (28%)
  starting transfers between devices  19.5 us (18%)
  Pallas kernels  5.97 us (6%)
  other arithmetic  1.9 us (2%)
    all_to_all x2, blocking collectives, to_each(): return lax.all_to_all(x, axes, split_axis=0, concat_axis=0, tiled=True)  48.3 us
    all_to_all x1, waiting for transfers between devices, to_each(): return lax.all_to_all(x, axes, split_axis=0, concat_axis=0, tiled=True)  30.2 us
    all_to_all x1, starting transfers between devices, to_each(): return lax.all_to_all(x, axes, split_axis=0, concat_axis=0, tiled=True)  19.5 us
    pallas_call x1, Pallas kernels, correlate(): pl.pallas_call(correlate_kernel, in_specs=[pl.BlockSpec(memory_space=pltp...  3.5 us
    pallas_call x1, Pallas kernels, gate(): pl.pallas_call(gate_kernel, grid=(chans // tile,), in_specs=[spec] * 4, o...  2.42 us
  transfers between devices with their start and end apart: 1, of which 1 were waited for; matrix products, arithmetic and copies ran while one was open for 1% of the time, Pallas kernels for 0%

profile of v5, /device:TPU:1, one launch (start us, length us, event | category | flops | bytes accessed | tf_op | source)
XLA Modules:
  0.0 105.9 jit_solution(10475548540954778572)
XLA Ops:
  0.0 2.4 %gate.1 = bf16[256,16,128]{2,1,0:T(8,128)(2,1)} custom-call(bf16[1,2048,128]{2,1,0:T(8,128)(2,1)} %k_ref.1, bf16[1,2048,128]{2,1,0:T(8,128)(2,1)} %v_ref.1, bf16[1,2048,128]{2,1,0:T(8,128)(2,1)} %q_ref.1, bf16[1,2048,128]{2,1,0:T(8,128)(2,1)} %g_ref.1), custom_call_target="tpu_custom_call" | custom-call | tf_op jit(solution)/shard_map/gate/pallas_call | solution.py:78
  2.4 0.0 copy-start
  2.4 0.0 copy-start.1
  2.4 0.0 copy-start.2
  2.4 0.0 copy-start.3
  2.5 19.5 %all-to-all-start = ((bf16[256,16,128]{2,1,0:T(8,128)(2,1)}), bf16[256,16,128]{2,1,0:T(8,128)(2,1)S(1)}, u32[]{:S(2)}, u32[]{:S(2)}) async-start(bf16[256,16,128]{2,1,0:T(8,128)(2,1)} %gate.1), calls=%async_computation | async-start | bytes 2097152 | tf_op jit(solution)/shard_map/all_to_all | solution.py:193
  22.0 0.8 dynamic-slice_negate_fusion
  22.7 0.1 exponential_multiply_fusion.window_ref
  22.8 30.2 %all-to-all-done = bf16[256,16,128]{2,1,0:T(8,128)(2,1)S(1)} async-done(((bf16[256,16,128]{2,1,0:T(8,128)(2,1)}), bf16[256,16,128]{2,1,0:T(8,128)(2,1)S(1)}, u32[]{:S(2)}, u32[]{:S(2)}) %all-to-all-start) | async-done | bytes 1048608 | tf_op jit(solution)/shard_map/all_to_all | solution.py:193
  53.0 0.0 copy-done
  53.0 0.0 copy-done.1
  53.0 0.0 copy-done.2
  53.0 0.0 copy-done.3
  53.0 3.5 %correlate.1 = bf16[3,16,8,128]{3,2,1,0:T(8,128)(2,1)S(1)} custom-call(bf16[16,16,16,128]{3,2,1,0:T(8,128)(2,1)S(1)} %bitcast.6, bf16[2,544,256]{2,1,0:T(8,128)(2,1)S(1)} %copy-done, bf16[2,256,256]{2,1,0:T(8,128)(2,1)S(1)} %copy-done.1, bf16[2,256,256]{2,1,0:T(8,128)(2,1)S(1)} %copy-done.2, f32[18,2,8,128]{3,2,1,0:T(8,128)S(1)} %copy-done.3), custom_call_target="tpu_custom_call" | custom-call | flops 2852126720 | bytes 3000000 | tf_op jit(solution)/shard_map/correlate/pallas_call | solution.py:153
  56.5 19.9 %all_to_all.15.parts_ref = bf16[3,16,8,128]{3,2,1,0:T(8,128)(2,1)S(1)} all-to-all(bf16[3,16,8,128]{3,2,1,0:T(8,128)(2,1)S(1)} %correlate.1), channel_id=1, replica_groups=mesh['y_lo'=4,'z_hi'=3,'z_lo'=4,'x'=4,'y_hi'=2,'core'=2] {'z_hi'}, dimensions={0} | all-to-all | bytes 196608 | tf_op jit(solution)/shard_map/all_to_all | solution.py:193
  76.5 28.4 %all_to_all.16 = bf16[256,8,128]{2,1,0:T(8,128)(2,1)S(1)} all-to-all(bf16[256,8,128]{2,1,0:T(8,128)(2,1)S(1)} %bitcast.5), channel_id=1, replica_groups=mesh['y_lo'=4,'z_hi'=3,'z_lo'=4,'x'=4,'y_hi'=2,'core'=2] {'y_lo','z_lo',..., dimensions={0} | all-to-all | bytes 1048576 | tf_op jit(solution)/shard_map/all_to_all | solution.py:193
  104.8 1.0 bitcast_convert_fusion
  (2 shorter events, 0.1 us)
Async XLA Ops:
  2.4 50.5 %copy-start = (bf16[2,544,256]{2,1,0:T(8,128)(2,1)S(1)}, bf16[2,544,256]{2,1,0:T(8,128)(2,1)}, u32[]{:S(2)}) copy-start(bf16[2,544,256]{2,1,0:T(8,128)(2,1)} %constant.48.clone.outer_ref) | copy-start | bytes 1671172
  2.4 50.6 %copy-start.1 = (bf16[2,256,256]{2,1,0:T(8,128)(2,1)S(1)}, bf16[2,256,256]{2,1,0:T(8,128)(2,1)}, u32[]{:S(2)}) copy-start(bf16[2,256,256]{2,1,0:T(8,128)(2,1)} %constant.49.clone.fwd_ref) | copy-start | bytes 786436
  2.4 50.6 %copy-start.2 = (bf16[2,256,256]{2,1,0:T(8,128)(2,1)S(1)}, bf16[2,256,256]{2,1,0:T(8,128)(2,1)}, u32[]{:S(2)}) copy-start(bf16[2,256,256]{2,1,0:T(8,128)(2,1)} %constant.50.clone.bwd_ref) | copy-start | bytes 786436
  2.4 50.5 %copy-start.3 = (f32[18,2,8,128]{3,2,1,0:T(8,128)S(1)}, f32[18,2,8,128]{3,2,1,0:T(8,128)}, u32[]{:S(2)}) copy-start(f32[18,2,8,128]{3,2,1,0:T(8,128)} %constant.51.clone.twist_ref) | copy-start | bytes 442372
  2.5 50.5 %all-to-all-start = ((bf16[256,16,128]{2,1,0:T(8,128)(2,1)}), bf16[256,16,128]{2,1,0:T(8,128)(2,1)S(1)}, u32[]{:S(2)}, u32[]{:S(2)}) async-start(bf16[256,16,128]{2,1,0:T(8,128)(2,1)} %gate.1), calls=%async_computation | async-start | bytes 2097152 | tf_op jit(solution)/shard_map/all_to_all | solution.py:193
